TPU v7x, 32 devices: a whole 2x2x4 slice. The times are simulated.
32 devices in a mesh: groups: 2 (over y), tensor: 4 (over z), adapter: 2 (over x), sub: 2 (over core).
Axes of the slice: x: 2, y: 2, z: 4, core: 2. Of those that a mesh axis runs over, the one named last changes fastest.
Arguments:
- hidden: bfloat16 [1024, 2, 8192], P(('groups', 'tensor')), parts along dimension 0, may hold values from -6 to 6
- output_weight: bfloat16 [8192, 8192], P('tensor', ('adapter', 'sub')), may hold values from -0.0625 to 0.0625
- adapter_down_weight: bfloat16 [8192, 4096], P(('adapter', 'sub'), 'tensor'), may hold values from -0.0625 to 0.0625
- adapter_up_weight: bfloat16 [4096, 8192], P('tensor', ('adapter', 'sub')), may hold values from -0.75 to 0.75
- adapter_storage_slot: int32 [128], P('groups'), parts along dimension 0, may hold values from 0 to 63, as said below
- request_adapter: int32 [1024], P('groups'), parts along dimension 0, may hold values from 0 to 63, as said below
Outputs:
- projected: bfloat16 [1024, 2, 8192], P(('groups', 'tensor'), None, ('adapter', 'sub')), parts along dimension 0
There are 2 independent parts, one for each index of `groups`. A program takes and returns all parts, laid end to end along the dimension named above; an argument that names none is the same for every part. Nothing has to cross between parts.
Inputs may be any that keep to these rules, and one draw needn't show every extreme that they name: `adapter_storage_slot`: each storage slot is taken by exactly one adapter. Holder of a row: adapter_storage_slot[request_adapter[r]] // 16. In each aligned block of 128 rows, at most 64 rows have the same holder, and in every draw one holder has exactly 64 rows in every block.
All inputs are finite; a program needn't handle non-finite values.
Results may differ from a plain program's by a relative error of at most 0.0085.
Values may be sent and summed in bfloat16 or wider, within the bound.
A program may use at most 192 MiB of HBM per device.

v0:
```python
import jax
import jax.numpy as jnp
from jax import lax
from jax.sharding import PartitionSpec as P

ADAPTER_RANK = 64
ADP_HOLD = 16


ADAPTER_SCALE = 0.5


def route_table(adapter_storage_slot, request_adapter, row_dev, holders, capacity):
    catalog = adapter_storage_slot.shape[0]
    matches = request_adapter[:, None] == jnp.arange(catalog, dtype=jnp.int32)[None, :]
    storage = jnp.sum(jnp.where(matches, adapter_storage_slot[None, :], 0), axis=1)
    owners = storage // ADP_HOLD
    local_adapter = storage - owners * ADP_HOLD
    sources = owners.shape[0] // row_dev
    owners = owners.reshape(sources, row_dev)
    member = (owners[:, :, None] == jnp.arange(holders, dtype=jnp.int32)[None, None, :]).astype(
        jnp.int32
    )
    position = jnp.sum((jnp.cumsum(member, axis=1) - 1) * member, axis=2)
    target = owners * capacity + position
    return (owners, position, target, local_adapter.reshape(sources, row_dev))


def local(
    hidden,
    output_weight,
    adapter_down_weight,
    adapter_up_weight,
    adapter_storage_slot,
    request_adapter,
):
    row_dev, step_count, model_width = hidden.shape
    shard_width, column_width = output_weight.shape
    holders = lax.axis_size("tensor")
    holder_index = lax.axis_index("tensor")
    group_index = lax.axis_index(("adapter", "sub"))
    width_of_block = adapter_down_weight.shape[0]
    capacity = 2 * row_dev // holders
    slot_count = holders * capacity
    owners, position, target, local_adapter = route_table(
        adapter_storage_slot, request_adapter, row_dev, holders, capacity
    )
    my_target = lax.dynamic_index_in_dim(target, holder_index, 0, keepdims=False)
    selector_mask = (jnp.arange(slot_count, dtype=jnp.int32)[:, None] == my_target[None, :]).astype(
        jnp.bfloat16
    )
    my_columns = lax.dynamic_slice_in_dim(hidden, group_index * width_of_block, width_of_block, 2)
    outgoing = jnp.einsum(
        "sr,rpk->spk", selector_mask, my_columns, preferred_element_type=jnp.float32
    ).astype(jnp.bfloat16)
    arrived = (
        (owners == holder_index)[:, None, :]
        & (position[:, None, :] == jnp.arange(capacity, dtype=jnp.int32)[None, :, None])
    ).astype(jnp.int32)
    adapter_onehot = (
        local_adapter[:, :, None] == jnp.arange(ADP_HOLD, dtype=jnp.int32)[None, None, :]
    ).astype(jnp.float32)
    slot_adapter = jnp.einsum("scr,sra->sca", arrived.astype(jnp.float32), adapter_onehot).reshape(
        slot_count, ADP_HOLD
    )
    picker = jnp.repeat(slot_adapter, ADAPTER_RANK, axis=1)
    projected_all = jnp.einsum(
        "snk,kq->snq",
        lax.all_to_all(outgoing, "tensor", split_axis=0, concat_axis=0, tiled=True),
        adapter_down_weight,
        preferred_element_type=jnp.float32,
    )
    masked = projected_all * picker[:, None, :]
    partial_rank = jnp.sum(masked.reshape(slot_count, -1, ADP_HOLD, ADAPTER_RANK), axis=2)
    rank_full_sum = lax.psum(partial_rank.astype(jnp.bfloat16), ("adapter", "sub")).astype(
        jnp.float32
    )
    rank_start_index = (ADAPTER_SCALE * rank_full_sum).astype(jnp.bfloat16)
    rank_spread_rows = (
        jnp.tile(rank_start_index, (1, 1, ADP_HOLD)) * picker.astype(jnp.bfloat16)[:, None, :]
    )
    adapter_delta = jnp.einsum(
        "ulx,xd->uld", rank_spread_rows, adapter_up_weight, preferred_element_type=jnp.float32
    )
    adapter_back_output = adapter_delta.astype(jnp.bfloat16)
    shard_rows = lax.all_gather(output_weight, "tensor", axis=0, tiled=True)
    shard_count = shard_rows.shape[0] // shard_width
    columns = hidden
    columns = columns.reshape(row_dev, step_count, shard_count, shard_width)
    weights = shard_rows.reshape(shard_count, shard_width, column_width)
    partials = jnp.einsum("rpnk,nkc->nrpc", columns, weights, preferred_element_type=jnp.float32)
    rounded = lax.optimization_barrier(partials.astype(jnp.bfloat16))
    base_output_sum = jnp.sum(rounded.astype(jnp.float32), axis=0)
    returned_output = lax.all_to_all(
        adapter_back_output, "tensor", split_axis=0, concat_axis=0, tiled=True
    )
    adapter_rows = jnp.einsum(
        "zm,zoi->moi", selector_mask, returned_output, preferred_element_type=jnp.float32
    )
    return (base_output_sum + adapter_rows).astype(jnp.bfloat16)


def solution(mesh):
    return jax.shard_map(
        local,
        mesh=mesh,
        in_specs=(
            P(("groups", "tensor"), None, None),
            P("tensor", ("adapter", "sub")),
            P(("adapter", "sub"), "tensor"),
            P("tensor", ("adapter", "sub")),
            P("groups"),
            P("groups"),
        ),
        out_specs=P(("groups", "tensor"), None, ("adapter", "sub")),
        check_vma=False,
    )
```

profile of v0, /device:TPU:0, one launch (start us, length us, event | category | flops | bytes accessed | tf_op | source)
XLA Modules:
  0.0 728.1 jit_solution(17848147343905934098)
XLA Ops:
  7.4 0.8 select_reduce_fusion.1
  8.2 0.1 fusion.21
  8.3 0.3 reduce_window_sum.11
  8.6 0.2 select_reduce_fusion
  8.8 2.0 constant_dynamic-slice_fusion
  10.8 1.0 convolution_convert_fusion
  11.8 3.5 copy.29
  15.3 6.3 all-to-all-start
  21.6 0.0 all-reduce.2.cloned.1.call-start
  21.6 0.1 fusion.22
  21.8 0.1 reshape.101
  21.9 0.1 broadcast_in_dim.16
  22.0 1.3 copy.32
  23.3 46.5 %all-to-all-done = bf16[256,2,2048]{2,1,0:T(2,128)(2,1)S(1)} async-done(((bf16[256,2,2048]{2,1,0:T(2,128)(2,1)}), bf16[256,2,2048]{2,1,0:T(2,128)(2,1)S(1)}, u32[]{:S(2)}, u32[]{:S(2)}) %all-to-all-start) | async-done | bytes 2097184 | tf_op jit(solution)/shard_map/all_to_all | solution.py:69
  69.8 6.5 fusion.15
  76.3 1.9 copy.33
  78.2 0.8 reduce_sum.42
  79.0 0.0 all-reduce.2.cloned.1.call-update
  79.0 0.2 all-gather.2.cloned.1.call-start
  79.2 0.3 all-gather.2.cloned.1.call-update
  79.6 7.6 %reshape.99 = bf16[128,2,4,2048]{3,2,1,0:T(4,128)(2,1)} reshape(bf16[128,2,8192]{2,1,0:T(2,128)(2,1)} %param.6) | data formatting | bytes 8388608 | tf_op jit(solution)/shard_map/reshape | solution.py:89
  87.2 22.2 %all-reduce.2.cloned.1.call-done = bf16[256,2,64]{0,2,1:T(8,128)(2,1)} async-done(((bf16[256,2,64]{0,2,1:T(8,128)(2,1)}), bf16[256,2,64]{0,2,1:T(8,128)(2,1)}) %all-reduce.2.cloned.1.call-update) | async-done | bytes 65552 | tf_op jit(solution)/shard_map/psum | solution.py:75
  109.4 0.9 multiply_convert_fusion
  110.3 0.1 bitcast_multiply_fusion
  110.4 4.6 fusion.9
  115.0 3.4 copy.35
  118.4 4.7 all-to-all-start.1
  123.1 563.3 %all-gather.2.cloned.1.call-done = bf16[8192,2048]{1,0:T(8,128)(2,1)} async-done(((bf16[2048,2048]{1,0:T(8,128)(2,1)}), bf16[8192,2048]{1,0:T(8,128)(2,1)}) %all-gather.2.cloned.1.call-update) | async-done | bytes 33554448 | tf_op jit(solution)/shard_map/all_gather | solution.py:86
  686.4 26.0 %fusion.6 = bf16[4,128,2,2048]{3,1,2,0:T(8,128)(2,1)} fusion(bf16[4,2048,2048,1]{2,1,3,0:T(8,128)(2,1)} %bitcast.56, bf16[128,2,4,2048]{3,2,1,0:T(4,128)(2,1)} %reshape.99), kind=kOutput, calls=%fused_computation.7 | convolution fusion | flops 8592031744 | bytes 41943040 | tf_op jit(solution)/shard_map/rpnk,nkc->nrpc/dot_general | solution.py:91
  712.4 3.2 convert_reduce_fusion
  715.6 0.0 all-to-all-done.1
  715.6 3.0 fusion.12
  718.6 2.0 copy.37
  (6 shorter events, 0.1 us)
Async XLA Ops:
  15.3 54.5 %all-to-all-start = ((bf16[256,2,2048]{2,1,0:T(2,128)(2,1)}), bf16[256,2,2048]{2,1,0:T(2,128)(2,1)S(1)}, u32[]{:S(2)}, u32[]{:S(2)}) async-start(bf16[256,2,2048]{2,1,0:T(2,128)(2,1)} %copy.29), calls=%async_computation | async-start | bytes 4194304 | tf_op jit(solution)/shard_map/all_to_all | solution.py:69
  21.6 87.8 %all-reduce.2.cloned.1.call-start = ((), (), s32[]{:S(2)}) async-start(), calls=%async_computation.3 | async-start | bytes 131072 | tf_op jit(solution)/shard_map/psum | solution.py:75
  79.0 607.4 %all-gather.2.cloned.1.call-start = ((), (), s32[]{:S(2)}) async-start(), calls=%async_computation.2 | async-start | bytes 41943040 | tf_op jit(solution)/shard_map/all_gather | solution.py:86
  118.4 597.2 %all-to-all-start.1 = ((bf16[256,2,2048]{2,1,0:T(2,128)(2,1)}), bf16[256,2,2048]{2,1,0:T(2,128)(2,1)}, u32[]{:S(2)}, u32[]{:S(2)}) async-start(bf16[256,2,2048]{2,1,0:T(2,128)(2,1)} %copy.35), calls=%async_computation.1 | async-start | bytes 4194304 | tf_op jit(solution)/shard_map/all_to_all | solution.py:94
Sparse Core Ops, SparseCore 0:
  79.1 30.2 all-reduce.1
Sparse Core Ops, SparseCore 1:
  81.0 605.3 all-gather.1
where the time goes:
time: 729 us; the launch traced here: 728 us
  waiting for transfers between devices  632 us (87%)
  matrix products  41.2 us (6%)
  local copies, waits for them, and re-layouts  22 us (3%)
  between operations  15 us (2%)
  starting transfers between devices  11.2 us (2%)
    all_gather x1, waiting for transfers between devices, local(): shard_rows = lax.all_gather(output_weight, 'tensor', axis=0, tiled=True)  563 us
    all_to_all x1, waiting for transfers between devices, local(): lax.all_to_all(outgoing, 'tensor', split_axis=0, concat_axis=0, tiled=True)  46.5 us
    dot_general x1, matrix products, local(): jnp.einsum('rpnk,nkc->nrpc', columns, weights, preferred_element_type=jnp...  26 us
    psum x1, waiting for transfers between devices, local(): lax.psum(partial_rank.astype(jnp.bfloat16), ('adapter', 'sub'))  22.2 us
  transfers between devices with their start and end apart: 4, of which 3 were waited for; matrix products, arithmetic and copies ran while one was open for 7% of the time, Pallas kernels for 0%

commit v1 on v0

v1 whole, which is shorter than its diff:
```python
import functools

import jax
import jax.numpy as jnp
from jax import lax
from jax.experimental import pallas as pl
from jax.experimental.pallas import tpu as pltpu
from jax.sharding import PartitionSpec as P

ADAPTER_RANK = 64
ADP_HOLD = 16
ADAPTER_SCALE = 0.5
CHUNKS = 2
LANES = 128
MESH = pl.DeviceIdType.MESH


def kernel(
    T, A, S, C,
    hq_in, ht_in, w_in, down_in, up_in, code_ref, out_ref,
    hq, ht, w, down, up, z, spread, acc, part, rb,
    load_sem, loc_sem, ag_send, ag_recv, bc_send, bc_recv, z_send, z_recv, rs_send, rs_recv,
):
    Q = A * S
    t = lax.axis_index("tensor")
    a = lax.axis_index("adapter")
    s = lax.axis_index("sub")
    q = a * S + s
    rows = hq.shape[1]
    M = rows // C
    N = w.shape[1]
    X = down.shape[1]
    root_a, root_s = t // S, t % S
    is_root = q == t
    in_column = s == root_s

    def chunk(c):
        return pl.ds(c * M, M)

    def when(cond):
        return pl.when(cond)

    loads = [
        pltpu.make_async_copy(hq_in, hq.at[t], load_sem.at[0]),
        pltpu.make_async_copy(down_in, down, load_sem.at[1]),
        pltpu.make_async_copy(ht_in, ht.at[t], load_sem.at[2]),
        pltpu.make_async_copy(w_in, w, load_sem.at[3]),
        pltpu.make_async_copy(up_in, up, load_sem.at[4]),
    ]
    for copy in loads:
        copy.start()

    barrier = pltpu.get_barrier_semaphore()

    @when(t > 0)
    def _():
        pl.semaphore_signal(barrier, inc=1, device_id={"tensor": t - 1}, device_id_type=MESH)

    @when(t < T - 1)
    def _():
        pl.semaphore_signal(barrier, inc=1, device_id={"tensor": t + 1}, device_id_type=MESH)

    for off in range(1, Q):
        peer = lax.rem(q + off, Q)
        pl.semaphore_signal(
            barrier, inc=1, device_id={"adapter": peer // S, "sub": peer % S}, device_id_type=MESH
        )
    pl.semaphore_wait(barrier, Q - 1 + (t + T - 1) // T + (T - 1 - t + T - 1) // T)

    def gather_copy(d, c, side, own=False):
        source = hq_in.at[chunk(c), :] if own else hq.at[d, chunk(c), :]
        return pltpu.make_async_remote_copy(
            src_ref=source,
            dst_ref=hq.at[d, chunk(c), :],
            send_sem=ag_send.at[side, d, c],
            recv_sem=ag_recv.at[d, c],
            device_id={"tensor": t + 1 if side else t - 1},
            device_id_type=MESH,
        )

    def gather_send(d, c, side, own=False):
        @when((t < T - 1) if side else (t > 0))
        def _():
            gather_copy(d, c, side, own).start()

    def spread_copy(d, c, k, source, target):
        return pltpu.make_async_remote_copy(
            src_ref=source.at[d, chunk(c), :],
            dst_ref=ht.at[d, chunk(c), :],
            send_sem=bc_send.at[k, d, c],
            recv_sem=bc_recv.at[d, c],
            device_id=target,
            device_id_type=MESH,
        )

    def column_target(k):
        return {"adapter": lax.rem(a + k, A)}

    def sibling_target(k):
        return {"sub": lax.rem(s + k, S)}

    def local_copy(d, c):
        return pltpu.make_async_copy(
            hq.at[d, chunk(c), :], ht.at[d, chunk(c), :], loc_sem.at[d, c]
        )

    def rank_copy(d, c, off):
        peer = lax.rem(q + off, Q)
        return pltpu.make_async_remote_copy(
            src_ref=z.at[q, d, chunk(c), :],
            dst_ref=z.at[q, d, chunk(c), :],
            send_sem=z_send.at[off, d, c],
            recv_sem=z_recv.at[q, d, c],
            device_id={"adapter": peer // S, "sub": peer % S},
            device_id_type=MESH,
        )

    def rank_wait(d, c, off):
        peer = lax.rem(q + off, Q)
        pltpu.make_async_remote_copy(
            src_ref=z.at[peer, d, chunk(c), :],
            dst_ref=z.at[peer, d, chunk(c), :],
            send_sem=z_send.at[off, d, c],
            recv_sem=z_recv.at[peer, d, c],
            device_id={"adapter": peer // S, "sub": peer % S},
            device_id_type=MESH,
        ).wait_recv()

    def low_rank(d, c):
        code = code_ref[d, chunk(c), :]
        value = hq[d, chunk(c), :]
        total = jnp.zeros((M, LANES), jnp.float32)
        wide = 256
        for j in range(X // wide):
            product = jnp.dot(
                value, down[:, j * wide:(j + 1) * wide], preferred_element_type=jnp.float32
            )
            holder = (lax.broadcasted_iota(jnp.int32, (M, wide), 1) + j * wide) // ADAPTER_RANK
            product = jnp.where(holder == code, product, 0.0)
            for k in range(wide // LANES):
                total = total + product[:, k * LANES:(k + 1) * LANES]
        z[q, d, chunk(c), :] = total.astype(jnp.bfloat16)

        @pl.loop(1, Q)
        def _(off):
            rank_copy(d, c, off).start()

    def base(d, c):
        tile = min(N, 512)

        @pl.loop(0, N // tile)
        def _(j):
            cols = pl.ds(pl.multiple_of(j * tile, tile), tile)
            acc[:, cols] = jnp.dot(
                ht[d, chunk(c), :], w[:, cols], preferred_element_type=jnp.float32
            )

    def finish(d, c):
        @pl.loop(1, Q)
        def _(off):
            rank_wait(d, c, off)

        low = jnp.zeros((M, LANES), jnp.float32)
        for k in range(Q):
            low = low + z[k, d, chunk(c), :].astype(jnp.float32)
        low = (low * ADAPTER_SCALE).astype(jnp.bfloat16)
        code = code_ref[d, chunk(c), :]
        for j in range(X // LANES):
            holder = (lax.broadcasted_iota(jnp.int32, (M, LANES), 1) + j * LANES) // ADAPTER_RANK
            spread[:, j * LANES:(j + 1) * LANES] = jnp.where(
                holder == code, low.astype(jnp.float32), 0.0
            ).astype(jnp.bfloat16)
        tile = min(N, 512)

        @pl.loop(0, N // tile)
        def _(j):
            cols = pl.ds(pl.multiple_of(j * tile, tile), tile)
            delta = jnp.dot(spread[...], up[:, cols], preferred_element_type=jnp.float32)
            part[d, chunk(c), cols] = (acc[:, cols] + delta).astype(jnp.bfloat16)

    def arrive(d, c, side):
        pltpu.make_async_remote_copy(
            src_ref=hq.at[d, chunk(c), :],
            dst_ref=hq.at[d, chunk(c), :],
            send_sem=ag_send.at[side, d, c],
            recv_sem=ag_recv.at[d, c],
            device_id={"tensor": lax.rem(t + 1, T)},
            device_id_type=MESH,
        ).wait_recv()
        gather_send(d, c, side)

        @when(is_root)
        def _():
            for k in range(1, A):
                spread_copy(d, c, k - 1, hq, column_target(k)).start()
            for k in range(1, S):
                spread_copy(d, c, A - 2 + k, hq, sibling_target(k)).start()
            local_copy(d, c).start()

    def features(d, c):
        @when(is_root)
        def _():
            local_copy(d, c).wait()

        @when(jnp.logical_not(is_root))
        def _():
            spread_copy(d, c, 0, ht, sibling_target(1)).wait_recv()

        @when(jnp.logical_and(in_column, jnp.logical_not(is_root)))
        def _():
            for k in range(1, S):
                spread_copy(d, c, A - 2 + k, ht, sibling_target(k)).start()

    def both_sides(dist, body):
        @when(t + dist < T)
        def _():
            body(t + dist, 0)

        @when(t - dist >= 0)
        def _():
            body(t - dist, 1)

    def gather_step(dist, c):
        both_sides(dist, lambda d, side: arrive(d, c, side))
        if isinstance(dist, int):
            pass
        both_sides(dist, lambda d, side: low_rank(d, c))

        def second(d, side):
            features(d, c)
            base(d, c)
            finish(d, c)

        both_sides(dist, second)

    def sum_copy(d, slot, c, side):
        return pltpu.make_async_remote_copy(
            src_ref=part.at[d, chunk(c), :],
            dst_ref=rb.at[slot, chunk(c), :],
            send_sem=rs_send.at[d, c],
            recv_sem=rs_recv.at[slot, c],
            device_id={"tensor": t + 1 if side else t - 1},
            device_id_type=MESH,
        )

    def sum_wait(slot, c):
        pltpu.make_async_remote_copy(
            src_ref=rb.at[slot, chunk(c), :],
            dst_ref=rb.at[slot, chunk(c), :],
            send_sem=rs_send.at[0, c],
            recv_sem=rs_recv.at[slot, c],
            device_id={"tensor": lax.rem(t + 1, T)},
            device_id_type=MESH,
        ).wait_recv()

    def add_arrived(d, c):
        sum_wait(d, c)
        part[d, chunk(c), :] = (
            part[d, chunk(c), :].astype(jnp.float32) + rb[d, chunk(c), :].astype(jnp.float32)
        ).astype(jnp.bfloat16)

    def sum_step(dist, c):
        @when(t + dist < T)
        def _():
            d = t + dist

            @when(t > 0)
            def _():
                add_arrived(d, c)

            sum_copy(d, d, c, 1).start()

        @when(t - dist >= 0)
        def _():
            d = t - dist

            @when(t < T - 1)
            def _():
                add_arrived(d, c)

            slot = jnp.where(dist == 1, T, d)
            sum_copy(d, slot, c, 0).start()

    def last(c):
        @when(t > 0)
        def _():
            sum_wait(t, c)

        @when(t < T - 1)
        def _():
            sum_wait(T, c)

        total = part[t, chunk(c), :].astype(jnp.float32)
        left = rb[t, chunk(c), :].astype(jnp.float32)
        right = rb[T, chunk(c), :].astype(jnp.float32)
        total = total + jnp.where(t > 0, left, 0.0) + jnp.where(t < T - 1, right, 0.0)
        out_ref[chunk(c), :] = total.astype(jnp.bfloat16)

    def own_sends(c):
        gather_send(t, c, 0, own=True)
        gather_send(t, c, 1, own=True)

    own_sends(0)
    loads[0].wait()
    loads[1].wait()
    for c in range(C):
        low_rank(t, c)
    loads[2].wait()
    loads[3].wait()
    loads[4].wait()
    for c in range(C):
        base(t, c)
        finish(t, c)

    for c in range(C):
        @pl.loop(1, T)
        def _(dist):
            if c > 0:
                sum_step(T - dist, c - 1)
            gather_step(dist, c)
            if c + 1 < C:
                @when(dist == 1)
                def _():
                    own_sends(c + 1)

        if c > 0:
            last(c - 1)

    @pl.loop(1, T)
    def _(dist):
        sum_step(T - dist, C - 1)

    last(C - 1)

    @pl.loop(0, T)
    def _(d):
        for c in range(C):
            @when(jnp.logical_and(d >= t, t > 0))
            def _():
                gather_copy(d, c, 0).wait_send()

            @when(jnp.logical_and(d <= t, t < T - 1))
            def _():
                gather_copy(d, c, 1).wait_send()

            @pl.loop(1, Q)
            def _(off):
                rank_copy(d, c, off).wait_send()

            @when(d != t)
            def _():
                sum_copy(d, d, c, 1).wait_send()

                @when(is_root)
                def _():
                    for k in range(1, A):
                        spread_copy(d, c, k - 1, hq, column_target(k)).wait_send()

                @when(in_column)
                def _():
                    for k in range(1, S):
                        spread_copy(d, c, A - 2 + k, ht, sibling_target(k)).wait_send()


def row_codes(adapter_storage_slot, request_adapter, steps):
    catalog = adapter_storage_slot.shape[0]
    matches = request_adapter[:, None] == jnp.arange(catalog, dtype=jnp.int32)[None, :]
    storage = jnp.sum(jnp.where(matches, adapter_storage_slot[None, :], 0), axis=1)
    local_slot = storage - lax.axis_index("tensor") * ADP_HOLD
    return jnp.repeat(local_slot, steps)


def local(
    hidden,
    output_weight,
    adapter_down_weight,
    adapter_up_weight,
    adapter_storage_slot,
    request_adapter,
):
    row_dev, steps, _ = hidden.shape
    T = lax.axis_size("tensor")
    A = lax.axis_size("adapter")
    S = lax.axis_size("sub")
    Q = A * S
    C = CHUNKS
    t = lax.axis_index("tensor")
    q = lax.axis_index(("adapter", "sub"))
    K, N = output_weight.shape
    KQ, X = adapter_down_weight.shape
    assert T == Q and K == KQ
    R = row_dev * steps
    hq = lax.dynamic_slice_in_dim(hidden, q * KQ, KQ, 2).reshape(R, KQ)
    ht = lax.dynamic_slice_in_dim(hidden, t * K, K, 2).reshape(R, K)
    codes = row_codes(adapter_storage_slot, request_adapter, steps).reshape(T, R, 1)
    bf = jnp.bfloat16
    dma = pltpu.SemaphoreType.DMA
    vmem = pl.BlockSpec(memory_space=pltpu.VMEM)
    anywhere = pl.BlockSpec(memory_space=pl.ANY)
    out = pl.pallas_call(
        functools.partial(kernel, T, A, S, C),
        out_shape=jax.ShapeDtypeStruct((R, N), bf),
        in_specs=[anywhere] * 5 + [vmem],
        out_specs=vmem,
        scratch_shapes=[
            pltpu.VMEM((T, R, KQ), bf),
            pltpu.VMEM((T, R, K), bf),
            pltpu.VMEM((K, N), bf),
            pltpu.VMEM((KQ, X), bf),
            pltpu.VMEM((X, N), bf),
            pltpu.VMEM((Q, T, R, LANES), bf),
            pltpu.VMEM((R // C, X), bf),
            pltpu.VMEM((R // C, N), jnp.float32),
            pltpu.VMEM((T, R, N), bf),
            pltpu.VMEM((T + 1, R, N), bf),
            dma((5,)),
            dma((T, C)),
            dma((2, T, C)),
            dma((T, C)),
            dma((A + S - 2, T, C)),
            dma((T, C)),
            dma((Q, T, C)),
            dma((Q, T, C)),
            dma((T, C)),
            dma((T + 1, C)),
        ],
        compiler_params=pltpu.CompilerParams(
            collective_id=0, has_side_effects=True, vmem_limit_bytes=56 * 1024 * 1024
        ),
        cost_estimate=pl.CostEstimate(
            flops=2 * T * R * (K * N + KQ * X + X * N),
            bytes_accessed=2 * (K * N + KQ * X + X * N + 4 * T * R * K),
            transcendentals=0,
        ),
    )(hq, ht, output_weight, adapter_down_weight, adapter_up_weight, codes)
    return out.reshape(row_dev, steps, N)


def solution(mesh):
    return jax.shard_map(
        local,
        mesh=mesh,
        in_specs=(
            P(("groups", "tensor"), None, None),
            P("tensor", ("adapter", "sub")),
            P(("adapter", "sub"), "tensor"),
            P("tensor", ("adapter", "sub")),
            P("groups"),
            P("groups"),
        ),
        out_specs=P(("groups", "tensor"), None, ("adapter", "sub")),
        check_vma=False,
    )
```

time: 729 us -> 163 us (0.22)
  waiting for transfers between devices: 632 us -> 0 us
  Pallas kernels: 0 us -> 151 us
  matrix products: 41.2 us -> 0 us
  between operations: 15 us -> 0.02 us
  starting transfers between devices: 11.2 us -> 0 us
  local copies, waits for them, and re-layouts: 22 us -> 10.9 us
    all_gather x1 -> x0, waiting for transfers between devices: 563 us -> none  [local(): shard_rows = lax.all_gather(output_weight, 'tensor', axis=0, tiled=True)]
    pallas_call x0 -> x1, Pallas kernels: none -> 151 us  [local(): pl.pallas_call(functools.partial(kernel, T, A, S, C), out_shape=jax.Shape...]
    all_to_all x2 -> x0, waiting for transfers between devices: 46.5 us -> none  [the longest x1 46.5 us: local(): lax.all_to_all(outgoing, 'tensor', split_axis=0, concat_axis=0, tiled=True)]
    dot_general x6 -> x0, matrix products: 41.2 us -> none  [the longest x1 26 us: local(): jnp.einsum('rpnk,nkc->nrpc', columns, weights, preferred_element_type=jnp...]
    psum x1 -> x0, waiting for transfers between devices: 22.2 us -> none  [local(): lax.psum(partial_rank.astype(jnp.bfloat16), ('adapter', 'sub'))]
    all_to_all x2 -> x0, starting transfers between devices: 11 us -> none  [the longest x1 6.32 us: local(): lax.all_to_all(outgoing, 'tensor', split_axis=0, concat_axis=0, tiled=True)]
    convert_element_type x4 -> x0, local copies, waits for them, and re-layouts: 9.04 us -> none  [the longest x1 3.51 us: local(): outgoing = jnp.einsum('sr,rpk->spk', selector_mask, my_columns, preferred...]
  transfers between devices with their start and end apart: 4 -> 0, of which waited for: 3 -> 0; matrix products, arithmetic and copies ran while one was open for 7% -> 0% of each run, Pallas kernels for 0% -> 0%
where the time goes in v1:
time: 163 us; the launch traced here: 162 us
  Pallas kernels  151 us (93%)
  local copies, waits for them, and re-layouts  10.9 us (7%)
    pallas_call x1, Pallas kernels, local(): pl.pallas_call(functools.partial(kernel, T, A, S, C), out_shape=jax.Shape...  151 us

profile of v1, /device:TPU:0, one launch (start us, length us, event | category | flops | bytes accessed | tf_op | source)
XLA Modules:
  0.0 162.5 jit_solution(9317747777903962686)
XLA Ops:
  0.0 0.8 select_reduce_fusion
  0.8 0.1 copy.10
  1.0 2.7 %copy.11.code_ref = s32[4,256,1]{2,1,0:T(8,128)} copy(s32[4,256,1]{0,1,2:T(8,128)S(1)} %bitcast.3) | data formatting | bytes 8192 | tf_op jit(solution)/shard_map/broadcast_in_dim | solution.py:370
  3.7 3.1 %constant_dynamic-slice_fusion = (bf16[128,2,2048]{2,1,0:T(2,128)(2,1)S(1)}, bf16[128,2,2048]{2,1,0:T(2,128)(2,1)S(1)}) fusion(bf16[128,2,8192]{2,1,0:T(2,128)(2,1)} %param.6, s32[]{:T(128)S(6)} %select_n.11, s32[]{:T(128)S(6)} %select_n.10), kind=kLoop, calls=%fused_computation.3 | loop fusion | bytes 4194312 | tf_op jit(solution)/shard_map/dynamic_slice | solution.py:394
  6.8 1.2 reshape.19.ht_in
  8.0 1.2 reshape.18.hq_in
  9.2 150.7 %shard_map.64 = bf16[256,2048]{1,0:T(8,128)(2,1)} custom-call(bf16[256,2048]{1,0:T(8,128)(2,1)} %reshape.18.hq_in, bf16[256,2048]{1,0:T(8,128)(2,1)} %reshape.19.ht_in, bf16[2048,2048]{1,0:T(8,128)(2,1)} %w_in.1, bf16[2048,1024]{1,0:T(8,128)(2,1)} %down_in.1, bf16[1024,2048]{1,0:T(8,128)(2,1)} %up_in.1, s32[4,256,1]{2,1,0:T(8,128)} %copy.11.code_ref), custom_call_target="tpu_custom_call" | custom-call | flops 17179869184 | bytes 33554432 | tf_op jit(solution)/shard_map/pallas_call | solution.py:400
  159.9 2.5 %reshape.20 = bf16[128,2,2048]{2,1,0:T(2,128)(2,1)} reshape(bf16[256,2048]{1,0:T(8,128)(2,1)} %shard_map.64) | data formatting | bytes 2097152 | tf_op jit(solution)/shard_map/reshape | solution.py:436
  (2 shorter events, 0.1 us)

commit v2 on v1

--- a/solution.py
+++ b/solution.py
@@ -126,6 +126,9 @@
             device_id_type=MESH,
         ).wait_recv()
 
+    def lane_holder(first):
+        return (lax.broadcasted_iota(jnp.int32, (M, LANES), 1) + first) // ADAPTER_RANK
+
     def low_rank(d, c):
         code = code_ref[d, chunk(c), :]
         value = hq[d, chunk(c), :]
@@ -135,10 +138,11 @@
             product = jnp.dot(
                 value, down[:, j * wide:(j + 1) * wide], preferred_element_type=jnp.float32
             )
-            holder = (lax.broadcasted_iota(jnp.int32, (M, wide), 1) + j * wide) // ADAPTER_RANK
-            product = jnp.where(holder == code, product, 0.0)
             for k in range(wide // LANES):
-                total = total + product[:, k * LANES:(k + 1) * LANES]
+                holder = lane_holder(j * wide + k * LANES)
+                total = total + jnp.where(
+                    holder == code, product[:, k * LANES:(k + 1) * LANES], 0.0
+                )
         z[q, d, chunk(c), :] = total.astype(jnp.bfloat16)
 
         @pl.loop(1, Q)
@@ -166,7 +170,7 @@
         low = (low * ADAPTER_SCALE).astype(jnp.bfloat16)
         code = code_ref[d, chunk(c), :]
         for j in range(X // LANES):
-            holder = (lax.broadcasted_iota(jnp.int32, (M, LANES), 1) + j * LANES) // ADAPTER_RANK
+            holder = lane_holder(j * LANES)
             spread[:, j * LANES:(j + 1) * LANES] = jnp.where(
                 holder == code, low.astype(jnp.float32), 0.0
             ).astype(jnp.bfloat16)
@@ -222,16 +226,17 @@
 
     def gather_step(dist, c):
         both_sides(dist, lambda d, side: arrive(d, c, side))
-        if isinstance(dist, int):
-            pass
         both_sides(dist, lambda d, side: low_rank(d, c))
 
-        def second(d, side):
-            features(d, c)
-            base(d, c)
-            finish(d, c)
-
-        both_sides(dist, second)
+    def feature_step(dist, c):
+        both_sides(dist, lambda d, side: features(d, c))
+
+    def project(d, c):
+        base(d, c)
+        finish(d, c)
+
+    def project_step(dist, c):
+        both_sides(dist, lambda d, side: project(d, c))
 
     def sum_copy(d, slot, c, side):
         return pltpu.make_async_remote_copy(
@@ -301,36 +306,49 @@
         gather_send(t, c, 1, own=True)
 
     own_sends(0)
-    loads[0].wait()
-    loads[1].wait()
-    for c in range(C):
-        low_rank(t, c)
-    loads[2].wait()
-    loads[3].wait()
-    loads[4].wait()
-    for c in range(C):
-        base(t, c)
-        finish(t, c)
+    for copy in loads:
+        copy.wait()
 
     for c in range(C):
         @pl.loop(1, T)
         def _(dist):
             if c > 0:
                 sum_step(T - dist, c - 1)
+
+            @when(dist > 1)
+            def _():
+                feature_step(dist - 1, c)
+
             gather_step(dist, c)
-            if c + 1 < C:
+            if c == 0:
                 @when(dist == 1)
                 def _():
+                    for k in range(C):
+                        low_rank(t, k)
+
+            if c + 1 < C:
+                @when(dist == max(T - 2, 1))
+                def _():
                     own_sends(c + 1)
 
-        if c > 0:
-            last(c - 1)
+            @when(dist > 1)
+            def _():
+                project_step(dist - 1, c)
+
+        feature_step(T - 1, c)
+        project_step(T - 1, c)
 
     @pl.loop(1, T)
     def _(dist):
         sum_step(T - dist, C - 1)
 
-    last(C - 1)
+        @when(dist == 1)
+        def _():
+            for c in range(C):
+                project(t, c)
+
+    for c in range(C):
+        last(c)
 
     @pl.loop(0, T)
     def _(d):
@@ -393,6 +411,7 @@
     hq = lax.dynamic_slice_in_dim(hidden, q * KQ, KQ, 2).reshape(R, KQ)
     ht = lax.dynamic_slice_in_dim(hidden, t * K, K, 2).reshape(R, K)
     codes = row_codes(adapter_storage_slot, request_adapter, steps).reshape(T, R, 1)
+    codes = jnp.broadcast_to(codes, (T, R, LANES))
     bf = jnp.bfloat16
     dma = pltpu.SemaphoreType.DMA
     vmem = pl.BlockSpec(memory_space=pltpu.VMEM)

time: 163 us -> 144 us (0.88)
  Pallas kernels: 151 us -> 132 us
    pallas_call x1, Pallas kernels: 151 us -> 132 us  [local(): pl.pallas_call(functools.partial(kernel, T, A, S, C), out_shape=jax.Shape...]
    broadcast_in_dim x2, local copies, waits for them, and re-layouts: 2.74 us -> 0.12 us  [row_codes(): return jnp.repeat(local_slot, steps)]
where the time goes in v2:
time: 144 us; the launch traced here: 142 us
  Pallas kernels  132 us (92%)
  local copies, waits for them, and re-layouts  9.32 us (6%)
    pallas_call x1, Pallas kernels, local(): pl.pallas_call(functools.partial(kernel, T, A, S, C), out_shape=jax.Shape...  132 us
    dynamic_slice x1, local copies, waits for them, and re-layouts, local(): ht = lax.dynamic_slice_in_dim(hidden, t * K, K, 2).reshape(R, K)  3.1 us

profile of v2, /device:TPU:0, one launch (start us, length us, event | category | flops | bytes accessed | tf_op | source)
XLA Modules:
  0.0 142.4 jit_solution(16245226410451158178)
XLA Ops:
  0.0 0.8 select_reduce_fusion
  0.8 0.1 copy.10
  1.0 0.1 copy.11
  1.0 1.0 broadcast_in_dim.29.code_ref
  2.1 3.1 %constant_dynamic-slice_fusion = (bf16[128,2,2048]{2,1,0:T(2,128)(2,1)S(1)}, bf16[128,2,2048]{2,1,0:T(2,128)(2,1)S(1)}) fusion(bf16[128,2,8192]{2,1,0:T(2,128)(2,1)} %param.6, s32[]{:T(128)S(6)} %select_n.11, s32[]{:T(128)S(6)} %select_n.10), kind=kLoop, calls=%fused_computation.3 | loop fusion | bytes 4194312 | tf_op jit(solution)/shard_map/dynamic_slice | solution.py:412
  5.2 1.2 reshape.19.ht_in
  6.4 1.2 reshape.18.hq_in
  7.6 132.3 %shard_map.64 = bf16[256,2048]{1,0:T(8,128)(2,1)} custom-call(bf16[256,2048]{1,0:T(8,128)(2,1)} %reshape.18.hq_in, bf16[256,2048]{1,0:T(8,128)(2,1)} %reshape.19.ht_in, bf16[2048,2048]{1,0:T(8,128)(2,1)} %w_in.1, bf16[2048,1024]{1,0:T(8,128)(2,1)} %down_in.1, bf16[1024,2048]{1,0:T(8,128)(2,1)} %up_in.1, s32[4,256,128]{2,1,0:T(8,128)} %broadcast_in_dim.29.code_ref), custom_call_target="tpu_custom_call" | custom-call | flops 17179869184 | bytes 33554432 | tf_op jit(solution)/shard_map/pallas_call | solution.py:419
  139.9 2.5 %reshape.20 = bf16[128,2,2048]{2,1,0:T(2,128)(2,1)} reshape(bf16[256,2048]{1,0:T(8,128)(2,1)} %shard_map.64) | data formatting | bytes 2097152 | tf_op jit(solution)/shard_map/reshape | solution.py:455
  (2 shorter events, 0.1 us)
